TPU v7x, 128 devices: a whole 4x4x4 slice. The times are simulated.
128 devices in a mesh: dp: 4 (over y_hi, core), expert: 8 (over y_lo, z), etp: 4 (over x).
Axes of the slice: x: 4, y: 4 (y_hi: 2, y_lo: 2; y = y_hi * 2 + y_lo), z: 4, core: 2. Of those that a mesh axis runs over, the one named last changes fastest.
Arguments:
- layer_input: bfloat16 [4096, 3072], P(('dp', 'expert'), 'etp'), may hold values from -6 to 6
- grad_output: bfloat16 [4096, 3072], P(('dp', 'expert'), 'etp'), may hold values from -6 to 6
- expert_ids: int32 [4096, 2], P(('dp', 'expert')), may hold values from 0 to 7, all different within a row; in each aligned block of 128 rows (0 to 127, 128 to 255, ...) at most 36 rows name the same one
- gate_probs: float32 [4096, 2], P(('dp', 'expert')), may hold values from 0.1 to 1
- up_weight: bfloat16 [8, 3072, 16384], P('expert', None, ('dp', 'etp')), may hold values from -0.15625 to 0.15625
- down_weight: bfloat16 [8, 16384, 3072], P('expert', ('dp', 'etp')), may hold values from -0.046875 to 0.046875
Outputs:
- grad_input: bfloat16 [4096, 3072], P(('dp', 'expert'), 'etp')
- grad_up: bfloat16 [8, 3072, 16384], P('expert', None, ('dp', 'etp'))
- grad_down: bfloat16 [8, 16384, 3072], P('expert', ('dp', 'etp'))
Inputs may be any that keep to these rules, and one draw needn't show every extreme that they name: `expert_ids`: among the 128 tokens of one index of dp+expert (aligned blocks of rows) no expert is named more than 36 times, a bound that some block reaches; the two picks of a token differ.
All inputs are finite; a program needn't handle non-finite values.
Results may differ from a plain program's by a relative error of at most 0.02.
Values may be sent and summed in bfloat16 or wider, within the bound.
A program may use at most 192 MiB of HBM per device.

v0:
```python
import jax
import jax.numpy as jnp
from jax import lax
from jax.sharding import PartitionSpec as P

inv_root_two = 0.7071067811865476
inv_root_tau = 0.3989422804014327


def gelu_value(value):
    return 0.5 * value * (1.0 + lax.erf(value * inv_root_two))


def gelu_slope(value):
    return (
        0.5 * (1.0 + lax.erf(value * inv_root_two))
        + value * jnp.exp(-0.5 * value * value) * inv_root_tau
    )


def slot_table(routes, experts, capacity):
    flat_ids = routes.reshape(-1)
    onehot = (flat_ids[:, None] == jnp.arange(experts, dtype=jnp.int32)[None, :]).astype(jnp.int32)
    before = jnp.cumsum(onehot, axis=0) - onehot
    position = jnp.sum(before * onehot, axis=1)
    return flat_ids * capacity + position


def expert_block(rows_x, rows_g, up_block, down_block):
    before_act = jnp.dot(rows_x, up_block, preferred_element_type=jnp.float32)
    hidden = gelu_value(before_act).astype(jnp.bfloat16)
    back_grad = lax.dot_general(
        rows_g, down_block, (((1,), (1,)), ((), ())), preferred_element_type=jnp.float32
    )
    pre_grad = (back_grad * gelu_slope(before_act)).astype(jnp.bfloat16)
    down_part = lax.dot_general(
        hidden, rows_g, (((0,), (0,)), ((), ())), preferred_element_type=jnp.float32
    )
    up_part = lax.dot_general(
        rows_x, pre_grad, (((0,), (0,)), ((), ())), preferred_element_type=jnp.float32
    )
    return (pre_grad, up_part, down_part)


def on_device(layer_input, grad_output, expert_ids, gate_probs, up_weight, down_weight):
    experts = lax.axis_size("expert")
    copies = lax.axis_size("dp")
    feature_parts = lax.axis_size("etp")
    tok_rows = layer_input.shape[0]
    quarter = layer_input.shape[1]
    capacity = min(tok_rows, 2 * tok_rows // experts + tok_rows // 32)
    group_rows = experts * capacity
    up_local = up_weight[0]
    down_local = down_weight[0]
    hidden_width = up_local.shape[1]
    slots = slot_table(expert_ids, experts, capacity)
    placing = (jnp.arange(group_rows, dtype=jnp.int32)[:, None] == slots[None, :]).astype(
        jnp.bfloat16
    )
    token_placing = jnp.sum(placing.reshape(group_rows, tok_rows, 2), axis=2)
    scaled = (grad_output.astype(jnp.float32)[:, None, :] * gate_probs[:, :, None]).astype(
        jnp.bfloat16
    )
    scaled = scaled.reshape(2 * tok_rows, quarter)
    send_x = jnp.dot(token_placing, layer_input, preferred_element_type=jnp.float32).astype(
        jnp.bfloat16
    )
    send_g = jnp.dot(placing, scaled, preferred_element_type=jnp.float32).astype(jnp.bfloat16)
    send_x = send_x.reshape(experts, capacity, quarter)
    send_g = send_g.reshape(experts, capacity, quarter)
    got_x, got_g = (
        lax.all_to_all(send_x, "expert", split_axis=0, concat_axis=0, tiled=True),
        lax.all_to_all(send_g, "expert", split_axis=0, concat_axis=0, tiled=True),
    )
    full_x, full_g = (
        lax.all_gather(got_x, "etp", axis=2, tiled=True),
        lax.all_gather(got_g, "etp", axis=2, tiled=True),
    )
    rows_x = full_x.reshape(group_rows, quarter * feature_parts)
    rows_g = full_g.reshape(group_rows, quarter * feature_parts)
    every_x, every_g = (
        lax.all_gather(rows_x, "dp", axis=0, tiled=True),
        lax.all_gather(rows_g, "dp", axis=0, tiled=True),
    )
    pre_grad, up_sum, down_sum = expert_block(every_x, every_g, up_local, down_local)
    up_split = up_local.reshape(feature_parts, quarter, hidden_width)
    grad_blocks = pre_grad.reshape(copies, group_rows, hidden_width)
    count_blocks = lax.axis_size(("dp", "etp")) * group_rows // group_rows
    block_index = jnp.arange(count_blocks, dtype=jnp.int32)
    chosen_rows = jnp.take(grad_blocks, block_index // feature_parts, axis=0)
    chosen_cols = jnp.take(up_split, block_index % feature_parts, axis=0)
    result = jnp.einsum(
        "brf,bqf->brq", chosen_rows, chosen_cols, preferred_element_type=jnp.float32
    )
    own_rows = lax.psum_scatter(
        result.reshape(count_blocks * group_rows, quarter).astype(jnp.bfloat16),
        ("dp", "etp"),
        scatter_dimension=0,
        tiled=True,
    ).astype(jnp.float32)
    returned = lax.all_to_all(
        own_rows.reshape(experts, capacity, quarter).astype(jnp.bfloat16),
        "expert",
        split_axis=0,
        concat_axis=0,
        tiled=True,
    ).astype(jnp.float32)
    picked = jnp.take(returned.reshape(group_rows, quarter), slots, axis=0).reshape(
        tok_rows, 2, quarter
    )
    grad_input = jnp.sum(picked, axis=1).astype(jnp.bfloat16)
    grad_up = up_sum.astype(jnp.bfloat16)[None]
    grad_down = down_sum.astype(jnp.bfloat16)[None]
    return (grad_input, grad_up, grad_down)


def solution(mesh):
    return jax.shard_map(
        on_device,
        mesh=mesh,
        in_specs=(
            P(("dp", "expert"), "etp"),
            P(("dp", "expert"), "etp"),
            P(("dp", "expert"), None),
            P(("dp", "expert"), None),
            P("expert", None, ("dp", "etp")),
            P("expert", ("dp", "etp"), None),
        ),
        out_specs=(
            P(("dp", "expert"), "etp"),
            P("expert", None, ("dp", "etp")),
            P("expert", ("dp", "etp"), None),
        ),
        check_vma=False,
    )
```

profile of v0, /device:TPU:0, one launch (start us, length us, event | category | flops | bytes accessed | tf_op | source)
XLA Modules:
  0.0 361.8 jit_solution(5310776368725623962)
XLA Ops:
  7.2 0.8 copy.20
  8.3 0.6 reduce-window.6
  8.9 0.2 slice_reduce_fusion
  9.5 0.7 compare_and_fusion.2
  10.3 0.3 convolution_convert_fusion.1
  10.6 16.1 %all_to_all.15 = bf16[8,36,768]{2,1,0:T(8,128)(2,1)} all-to-all(bf16[8,36,768]{2,1,0:T(8,128)(2,1)S(1)} %reshape.199), channel_id=1, replica_groups=mesh['dp'=4,'expert'=8,'etp'=4] {'expert'}, dimensions={0} | all-to-all | bytes 884736 | tf_op jit(solution)/shard_map/all_to_all | solution.py:72
  26.8 0.8 copy.24
  27.7 1.1 mul.88
  28.8 0.5 mul.89
  29.4 0.4 convolution_convert_fusion
  29.8 11.6 %all_to_all.16 = bf16[8,36,768]{2,1,0:T(8,128)(2,1)} all-to-all(bf16[8,36,768]{2,1,0:T(8,128)(2,1)S(1)} %reshape.197), channel_id=1, replica_groups=mesh['dp'=4,'expert'=8,'etp'=4] {'expert'}, dimensions={0} | all-to-all | bytes 884736 | tf_op jit(solution)/shard_map/all_to_all | solution.py:73
  41.5 14.0 %all-gather.9.cloned.1.call-done = bf16[8,36,3072]{2,1,0:T(8,128)(2,1)} async-done(((bf16[8,36,768]{2,1,0:T(8,128)(2,1)}), bf16[8,36,3072]{2,1,0:T(8,128)(2,1)}) %all-gather.9.cloned.1.call-update) | async-done | bytes 1769488 | tf_op jit(solution)/shard_map/all_gather | solution.py:76
  55.5 2.6 reshape.200
  58.2 28.8 %all-gather.5.cloned.1.call-done = bf16[8,36,3072]{2,1,0:T(8,128)(2,1)} async-done(((bf16[8,36,768]{2,1,0:T(8,128)(2,1)}), bf16[8,36,3072]{2,1,0:T(8,128)(2,1)}) %all-gather.5.cloned.1.call-update) | async-done | bytes 1769488 | tf_op jit(solution)/shard_map/all_gather | solution.py:77
  86.9 2.6 reshape.198
  89.5 0.2 reduce-scatter.2.cloned.1.call-start
  89.8 14.4 %gather_fusion.1 = bf16[16,768,1024]{2,1,0:T(8,128)(2,1)} fusion(bf16[4,768,1024]{2,1,0:T(8,128)(2,1)} %bitcast.38, s32[1024]{0:T(1024)S(1)} %pad_clamp_fusion.1), kind=kCustom, calls=%fused_computation.1 | custom fusion | bytes 50331712 | tf_op jit(solution)/shard_map/jit(_take)/gather | solution.py:91
  104.2 39.9 %all-gather.11.cloned.1.call-done = bf16[1152,3072]{1,0:T(8,128)(2,1)} async-done(((bf16[288,3072]{1,0:T(8,128)(2,1)}), bf16[1152,3072]{1,0:T(8,128)(2,1)}) %all-gather.11.cloned.1.call-update) | async-done | bytes 7077904 | tf_op jit(solution)/shard_map/all_gather | solution.py:82
  144.1 12.9 %fusion.11 = f32[1152,1024]{1,0:T(8,128)} fusion(bf16[1152,3072]{1,0:T(8,128)(2,1)} %all-gather.11.cloned.1.call-done, bf16[1,3072,1024]{2,1,0:T(8,128)(2,1)} %param.10), kind=kOutput, calls=%fused_computation.11 | convolution fusion | flops 7247757312 | bytes 18087936 | tf_op jit(solution)/shard_map/dot_general | solution.py:30
  157.1 43.5 %all-gather.7.cloned.1.call-done = bf16[1152,3072]{1,0:T(8,128)(2,1)} async-done(((bf16[288,3072]{1,0:T(8,128)(2,1)}), bf16[1152,3072]{1,0:T(8,128)(2,1)}) %all-gather.7.cloned.1.call-update) | async-done | bytes 7077904 | tf_op jit(solution)/shard_map/all_gather | solution.py:83
  200.6 13.8 %fusion.23 = bf16[1152,1024]{1,0:T(8,128)(2,1)S(1)} fusion(f32[1152,1024]{1,0:T(8,128)} %fusion.11, bf16[1152,3072]{1,0:T(8,128)(2,1)} %all-gather.7.cloned.1.call-done, bf16[1,1024,3072]{2,1,0:T(8,128)(2,1)} %param.11), kind=kOutput, calls=%fused_computation.25 | convolution fusion | flops 7259553792 | bytes 20447232 | tf_op jit(solution)/shard_map/dot_general | solution.py:32
  214.4 5.2 %gather_fusion = bf16[16,288,1024]{2,1,0:T(8,128)(2,1)} fusion(bf16[4,288,1024]{2,1,0:T(8,128)(2,1)S(1)} %bitcast.39, s32[1024]{0:T(1024)S(1)} %pad_clamp_fusion.2), kind=kCustom, calls=%fused_computation | custom fusion | bytes 18874432 | tf_op jit(solution)/shard_map/jit(_take)/gather | solution.py:90
  219.6 19.2 %fusion.6 = bf16[16,288,768]{2,1,0:T(8,128)(2,1)} fusion(bf16[16,768,1024]{2,1,0:T(8,128)(2,1)} %gather_fusion.1, pred[16]{0:T(512)(128)(4,1)S(1)} %get-tuple-element.5, bf16[16,288,1024]{2,1,0:T(8,128)(2,1)} %gather_fusion, pred[16]{0:T(512)(128)(4,1)S(1)} %get-tuple-element.6), kind=kOutput, calls=%fused_computation.10 | convolution fusion | flops 7268597760 | bytes 41680928 | tf_op jit(solution)/shard_map/brf,bqf->brq/dot_general | solution.py:92
  238.8 0.7 copy-done.2
  239.9 13.5 %convert_bitcast_fusion.1 = bf16[1,3072,1024]{2,1,0:T(8,128)(2,1)} fusion(bf16[1152,3072]{1,0:T(8,128)(2,1)} %all-gather.11.cloned.1.call-done, bf16[1152,1024]{1,0:T(8,128)(2,1)S(1)} %fusion.23), kind=kOutput, calls=%fused_computation.16 | convolution fusion | flops 7250903040 | bytes 15728640 | tf_op jit(solution)/shard_map/dot_general | solution.py:39
  253.5 77.9 %reduce-scatter.2.cloned.1.call-done = bf16[288,768]{1,0:T(8,128)(2,1)} async-done(((bf16[4608,768]{1,0:T(8,128)(2,1)}), bf16[288,768]{1,0:T(8,128)(2,1)}) %reduce-scatter.2.cloned.1.call-update) | async-done | bytes 442384 | tf_op jit(solution)/shard_map/reduce_scatter | solution.py:95
  331.3 1.9 convert_element_type.63
  333.2 4.5 %all-to-all-start.2 = ((bf16[8,36,768]{2,1,0:T(8,128)(2,1)}), bf16[8,36,768]{2,1,0:T(8,128)(2,1)S(1)}, u32[]{:S(2)}, u32[]{:S(2)}) async-start(bf16[8,36,768]{2,1,0:T(8,128)(2,1)} %convert_element_type.63), calls=%async_computation.3 | async-start | bytes 983040 | tf_op jit(solution)/shard_map/all_to_all | solution.py:101
  337.7 14.1 %convert_bitcast_fusion = bf16[1,1024,3072]{2,1,0:T(8,128)(2,1)} fusion(bf16[1152,3072]{1,0:T(8,128)(2,1)} %all-gather.7.cloned.1.call-done, f32[1152,1024]{1,0:T(8,128)} %fusion.11), kind=kOutput, calls=%fused_computation.15 | convolution fusion | flops 7256801280 | bytes 18087936 | tf_op jit(solution)/shard_map/dot_general | solution.py:36
  351.9 1.1 gather_fusion.2
  353.0 0.5 gather.17
  353.5 1.8 select_reduce_fusion
  (40 shorter events, 1.8 us)
Async XLA Ops:
  7.2 3.1 copy-start
  7.2 48.3 %all-gather.9.cloned.1.call-start = ((), (), s32[]{:S(2)}) async-start(), calls=%async_computation.6 | async-start | bytes 2457600 | tf_op jit(solution)/shard_map/all_gather | solution.py:76
  26.7 60.2 %all-gather.5.cloned.1.call-start = ((), (), s32[]{:S(2)}) async-start(), calls=%async_computation.4 | async-start | bytes 2457600 | tf_op jit(solution)/shard_map/all_gather | solution.py:77
  41.5 102.7 %all-gather.11.cloned.1.call-start = ((), (), s32[]{:S(2)}) async-start(), calls=%async_computation.7 | async-start | bytes 8847360 | tf_op jit(solution)/shard_map/all_gather | solution.py:82
  58.1 142.4 %all-gather.7.cloned.1.call-start = ((), (), s32[]{:S(2)}) async-start(), calls=%async_computation.5 | async-start | bytes 8847360 | tf_op jit(solution)/shard_map/all_gather | solution.py:83
  89.5 241.8 %reduce-scatter.2.cloned.1.call-start = ((), (), s32[]{:S(2)}) async-start(), calls=%async_computation.8 | async-start | bytes 7520256 | tf_op jit(solution)/shard_map/reduce_scatter | solution.py:95
  238.8 0.7 copy-start.2
  333.2 18.6 %all-to-all-start.2 = ((bf16[8,36,768]{2,1,0:T(8,128)(2,1)}), bf16[8,36,768]{2,1,0:T(8,128)(2,1)S(1)}, u32[]{:S(2)}, u32[]{:S(2)}) async-start(bf16[8,36,768]{2,1,0:T(8,128)(2,1)} %convert_element_type.63), calls=%async_computation.3 | async-start | bytes 983040 | tf_op jit(solution)/shard_map/all_to_all | solution.py:101
  337.7 17.5 %copy-start.1 = (bf16[128,768]{1,0:T(8,128)(2,1)S(1)}, bf16[128,768]{1,0:T(8,128)(2,1)}, u32[]{:S(2)}) copy-start(bf16[128,768]{1,0:T(8,128)(2,1)} %param.6) | copy-start | bytes 589828
Sparse Core Ops, SparseCore 0:
  26.8 28.6 all-gather.8
  57.2 29.7 all-gather.4
  89.2 54.8 all-gather.10
  146.2 54.2 all-gather.6
  239.0 92.3 reduce-scatter.1
where the time goes:
time: 363 us; the launch traced here: 362 us
  waiting for transfers between devices  204 us (56%)
  matrix products  74.2 us (20%)
  local copies, waits for them, and re-layouts  33.6 us (9%)
  blocking collectives  27.7 us (8%)
  between operations  14 us (4%)
  starting transfers between devices  4.86 us (1%)
    reduce_scatter x1, waiting for transfers between devices, on_device(): lax.psum_scatter(result.reshape(count_blocks * group_rows, quarter).astyp...  77.9 us
    all_gather x1, waiting for transfers between devices, on_device(): lax.all_gather(rows_g, 'dp', axis=0, tiled=True)  43.5 us
    all_gather x1, waiting for transfers between devices, on_device(): lax.all_gather(rows_x, 'dp', axis=0, tiled=True)  39.9 us
    all_gather x1, waiting for transfers between devices, on_device(): lax.all_gather(got_g, 'etp', axis=2, tiled=True)  28.8 us
    dot_general x1, matrix products, on_device(): jnp.einsum('brf,bqf->brq', chosen_rows, chosen_cols, preferred_element_ty...  19.2 us
    all_to_all x1, blocking collectives, on_device(): lax.all_to_all(send_x, 'expert', split_axis=0, concat_axis=0, tiled=True)  16.1 us
    gather x1, local copies, waits for them, and re-layouts, on_device(): chosen_cols = jnp.take(up_split, block_index % feature_parts, axis=0)  14.4 us
    dot_general x1, matrix products, expert_block(): lax.dot_general(hidden, rows_g, (((0,), (0,)), ((), ())), preferred_eleme...  14.1 us
  transfers between devices with their start and end apart: 6, of which 5 were waited for; matrix products, arithmetic and copies ran while one was open for 18% of the time, Pallas kernels for 0%

commit v1 on v0

v1 whole, which is shorter than its diff:
```python
import jax
import jax.numpy as jnp
from jax import lax
from jax.experimental import pallas as pl
from jax.experimental.pallas import tpu as pltpu
from jax.sharding import PartitionSpec as P

inv_root_two = 0.7071067811865476
inv_root_tau = 0.3989422804014327
MESH = pl.DeviceIdType.MESH
bf16 = jnp.bfloat16
f32 = jnp.float32

TOK = 128
QUARTER = 768
CAP = 36
BLOCK = 4 * CAP
CHUNK = 2 * BLOCK
ROWS = 4 * CHUNK
D = 3072
F = 1024
TILE = 256
HALF = QUARTER // 2
OFFSETS = (0, 3, 1, 2)
N_SEMS = 80


def kernel(
    x_ref, g_ref, meta_ref, up_hbm, down_hbm,
    gi_ref, gup_hbm, gdown_hbm,
    rows_x, rows_g, up, down, hid, pre, dense_x, dense_g, meta, place, pk_x, pk_g,
    dx, r1, r2a, r2b, zret, yd, y1, y2,
    ssem, rsem, wsem, osem,
):
    dp = lax.axis_index("dp")
    ex = lax.axis_index("expert")
    x = lax.axis_index("etp")
    c = dp % 2
    yl = ex // 4
    z = ex % 4
    y = (dp // 2) * 2 + yl

    def device(x_, y_, z_, c_):
        return ((y_ // 2) * 2 + c_, (y_ % 2) * 4 + z_, x_)

    xp, xm, xo = (x + 1) % 4, (x + 3) % 4, (x + 2) % 4
    yp, ym, yo = (y + 1) % 4, (y + 3) % 4, (y + 2) % 4
    to_xp, to_xm = device(xp, y, z, c), device(xm, y, z, c)
    to_yp, to_ym = device(x, yp, z, c), device(x, ym, z, c)
    to_core = device(x, y, z, 1 - c)
    to_z = {d: device(x, y, (z + d) % 4, c) for d in (1, 2, 3)}

    sent = []

    def send(src, dst, to):
        i = len(sent)
        copy = pltpu.make_async_remote_copy(
            src_ref=src, dst_ref=dst, send_sem=ssem.at[i], recv_sem=rsem.at[i],
            device_id=to, device_id_type=MESH,
        )
        copy.start()
        sent.append(copy)
        return copy

    load_up = pltpu.make_async_copy(up_hbm.at[0], up, wsem.at[0])
    load_down = pltpu.make_async_copy(down_hbm.at[0], down, wsem.at[1])
    load_up.start()
    load_down.start()

    partners = (to_xp, to_xm, to_yp, to_ym, to_core, to_z[1], to_z[2], to_z[3])
    barrier = pltpu.get_barrier_semaphore()
    for partner in partners:
        pl.semaphore_signal(barrier, inc=1, device_id=partner, device_id_type=MESH)
    pl.semaphore_wait(barrier, len(partners))

    def tok(y_):
        return pl.ds(pl.multiple_of(y_ * TOK, TOK), TOK)

    a_xp = send(x_ref, dense_x.at[tok(y)], to_yp)
    a_mp = send(meta_ref, meta.at[y], to_yp)
    a_gm = send(g_ref, dense_g.at[tok(y)], to_ym)
    a_mm = send(meta_ref, meta.at[y], to_ym)
    a_xm = send(x_ref, dense_x.at[tok(y)], to_ym)
    a_gp = send(g_ref, dense_g.at[tok(y)], to_yp)
    dense_x[tok(y), :] = x_ref[...]
    dense_g[tok(y), :] = g_ref[...]
    meta[y] = meta_ref[...]
    a_xp.wait_recv()
    b_x = send(dense_x.at[tok(ym)], dense_x.at[tok(ym)], to_yp)
    a_mp.wait_recv()
    b_m = send(meta.at[ym], meta.at[ym], to_yp)
    a_gm.wait_recv()
    b_g = send(dense_g.at[tok(yp)], dense_g.at[tok(yp)], to_ym)
    for copy in (a_mm, b_m):
        copy.wait_recv()

    row = lax.broadcasted_iota(jnp.int32, (4 * BLOCK, TOK), 0).astype(f32)
    gate = jnp.zeros((4 * BLOCK, 1), f32)
    for t in range(4):
        m = meta[t]
        first = row == jnp.where(yl == 0, m[0:1], m[2:3])
        second = row == jnp.where(yl == 0, m[1:2], m[3:4])
        hits = jnp.where(first, 1.0, 0.0) + jnp.where(second, 1.0, 0.0)
        place[:, t * TOK:(t + 1) * TOK] = hits.astype(bf16)
        gates = jnp.where(first, m[4:5], 0.0) + jnp.where(second, m[5:6], 0.0)
        gate = gate + jnp.sum(gates, axis=1, keepdims=True)
    for copy in (a_xm, a_gp, b_x, b_g):
        copy.wait_recv()
    pk_x[...] = jnp.dot(place[...], dense_x[...], preferred_element_type=f32).astype(bf16)
    pk_g[...] = (jnp.dot(place[...], dense_g[...], preferred_element_type=f32) * gate).astype(bf16)

    def packed(z_):
        return pl.ds(pl.multiple_of(z_ * BLOCK, BLOCK), BLOCK)

    def block(z_, c_):
        return pl.ds(pl.multiple_of((z_ * 2 + c_) * BLOCK, BLOCK), BLOCK)

    def chunk(z_):
        return pl.ds(pl.multiple_of(z_ * CHUNK, CHUNK), CHUNK)

    def part(x_):
        return pl.ds(pl.multiple_of(x_ * QUARTER, QUARTER), QUARTER)

    z_in = {}
    for d in (1, 3, 2):
        there = packed((z + d) % 4)
        here = (block(z, c), part(x))
        z_in[d] = (
            send(pk_x.at[there], rows_x.at[here], to_z[d]),
            send(pk_g.at[there], rows_g.at[here], to_z[d]),
        )
    rows_x[block(z, c), part(x)] = pk_x[packed(z), :]
    rows_g[block(z, c), part(x)] = pk_g[packed(z), :]

    zs = [(z + o) % 4 for o in OFFSETS]
    x_in = {}
    fwd = {}
    c_in = {}
    r1_in = {}
    r2a_in = {}
    r2b_in = {}
    rz_in = []

    def x_send(j):
        if j > 0:
            for copy in z_in[(4 - OFFSETS[j]) % 4]:
                copy.wait_recv()
        at = (block(zs[j], c), part(x))
        x_in[j] = (
            send(rows_x.at[at], rows_x.at[at], to_xp),
            send(rows_g.at[at], rows_g.at[at], to_xm),
            send(rows_x.at[at], rows_x.at[at], to_xm),
            send(rows_g.at[at], rows_g.at[at], to_xp),
        )

    def x_forward(j):
        x_in[j][0].wait_recv()
        at = (block(zs[j], c), part(xm))
        one = send(rows_x.at[at], rows_x.at[at], to_xp)
        x_in[j][1].wait_recv()
        at = (block(zs[j], c), part(xp))
        two = send(rows_g.at[at], rows_g.at[at], to_xm)
        fwd[j] = (one, two)

    def core_send(j):
        for copy in (x_in[j][2], x_in[j][3]) + fwd[j]:
            copy.wait_recv()
        at = block(zs[j], c)
        c_in[j] = (
            send(rows_x.at[at], rows_x.at[at], to_core),
            send(rows_g.at[at], rows_g.at[at], to_core),
        )

    def hidden_of(j):
        for copy in c_in[j]:
            copy.wait_recv()
        rows = chunk(zs[j])

        @pl.loop(0, F // TILE)
        def _(n):
            cols = pl.ds(pl.multiple_of(n * TILE, TILE), TILE)
            act = jnp.dot(rows_x[rows, :], up[:, cols], preferred_element_type=f32)
            back = lax.dot_general(
                rows_g[rows, :], down[cols, :], (((1,), (1,)), ((), ())),
                preferred_element_type=f32,
            )
            half_cdf = 0.5 * (1.0 + lax.erf(act * inv_root_two))
            hid[rows, cols] = (act * half_cdf).astype(bf16)
            slope = half_cdf + act * jnp.exp(-0.5 * act * act) * inv_root_tau
            pre[rows, cols] = (back * slope).astype(bf16)

    def input_grad_of(j):
        rows = chunk(zs[j])

        @pl.loop(0, D // TILE)
        def _(n):
            cols = pl.ds(pl.multiple_of(n * TILE, TILE), TILE)
            dx[rows, cols] = lax.dot_general(
                pre[rows, :], up[cols, :], (((1,), (1,)), ((), ())),
                preferred_element_type=f32,
            ).astype(bf16)

        r1_in[j] = send(dx.at[block(zs[j], 1 - c)], r1.at[j], to_core)

    def add_core(j):
        r1_in[j].wait_recv()
        rows = block(zs[j], c)
        dx[rows, :] = (dx[rows, :].astype(f32) + r1[j].astype(f32)).astype(bf16)
        start = pl.multiple_of(xo * QUARTER, HALF)
        r2a_in[j] = (
            send(dx.at[rows, pl.ds(start, HALF)], r2a.at[j, 0], to_xp),
            send(dx.at[rows, pl.ds(pl.multiple_of(start + HALF, HALF), HALF)], r2a.at[j, 1], to_xm),
        )

    def add_far(j):
        rows = block(zs[j], c)
        r2a_in[j][0].wait_recv()
        cols = pl.ds(pl.multiple_of(xp * QUARTER, HALF), HALF)
        dx[rows, cols] = (dx[rows, cols].astype(f32) + r2a[j, 0].astype(f32)).astype(bf16)
        one = send(dx.at[rows, part(xp)], r2b.at[j, 0], to_xp)
        r2a_in[j][1].wait_recv()
        cols = pl.ds(pl.multiple_of(xm * QUARTER + HALF, HALF), HALF)
        dx[rows, cols] = (dx[rows, cols].astype(f32) + r2a[j, 1].astype(f32)).astype(bf16)
        two = send(dx.at[rows, part(xm)], r2b.at[j, 1], to_xm)
        r2b_in[j] = (one, two)

    def add_near(j):
        rows = block(zs[j], c)
        for copy in r2b_in[j]:
            copy.wait_recv()
        total = (
            dx[rows, part(x)].astype(f32) + r2b[j, 0].astype(f32) + r2b[j, 1].astype(f32)
        ).astype(bf16)
        if OFFSETS[j] == 0:
            zret[packed(z), :] = total
        else:
            dx[rows, part(x)] = total
            rz_in.append(
                send(dx.at[rows, part(x)], zret.at[packed(z)], to_z[OFFSETS[j]])
            )

    stores = []

    def down_tiles(first, last):
        @pl.loop(first, last)
        def _(n):
            cols = pl.ds(pl.multiple_of(n * TILE, TILE), TILE)
            for k in range(D // F):
                wide = slice(k * F, (k + 1) * F)
                down[cols, wide] = lax.dot_general(
                    hid[:, cols], rows_g[:, wide], (((0,), (0,)), ((), ())),
                    preferred_element_type=f32,
                ).astype(bf16)

        rows = slice(first * TILE, last * TILE)
        store = pltpu.make_async_copy(down.at[rows], gdown_hbm.at[0, rows], osem.at[len(stores)])
        store.start()
        stores.append(store)

    def up_tiles(first, last):
        @pl.loop(first, last)
        def _(n):
            cols = pl.ds(pl.multiple_of(n * TILE, TILE), TILE)
            up[cols, :] = lax.dot_general(
                rows_x[:, cols], pre[...], (((0,), (0,)), ((), ())),
                preferred_element_type=f32,
            ).astype(bf16)

        rows = slice(first * TILE, last * TILE)
        store = pltpu.make_async_copy(up.at[rows], gup_hbm.at[0, rows], osem.at[len(stores)])
        store.start()
        stores.append(store)

    x_send(0)
    x_send(1)
    load_up.wait()
    load_down.wait()
    x_forward(0)
    core_send(0)
    x_send(2)
    hidden_of(0)
    x_forward(1)
    input_grad_of(0)
    core_send(1)
    x_send(3)
    hidden_of(1)
    x_forward(2)
    add_core(0)
    input_grad_of(1)
    core_send(2)
    add_far(0)
    hidden_of(2)
    x_forward(3)
    add_near(0)
    add_core(1)
    input_grad_of(2)
    core_send(3)
    add_far(1)
    hidden_of(3)
    add_near(1)
    add_core(2)
    input_grad_of(3)
    add_far(2)
    down_tiles(0, 1)
    add_near(2)
    add_core(3)
    down_tiles(1, 2)
    add_far(3)
    down_tiles(2, 4)
    add_near(3)
    up_tiles(0, 4)

    for copy in rz_in:
        copy.wait_recv()
    yd[...] = lax.dot_general(
        place[...], zret[...], (((0,), (0,)), ((), ())), preferred_element_type=f32
    ).astype(bf16)
    low, high = slice(0, HALF), slice(HALF, QUARTER)
    y1_in = (
        send(yd.at[tok(yo), low], y1.at[0], to_yp),
        send(yd.at[tok(yo), high], y1.at[1], to_ym),
    )
    up_tiles(4, 8)
    y1_in[0].wait_recv()
    yd[tok(yp), low] = (yd[tok(yp), low].astype(f32) + y1[0].astype(f32)).astype(bf16)
    y2_p = send(yd.at[tok(yp)], y2.at[0], to_yp)
    y1_in[1].wait_recv()
    yd[tok(ym), high] = (yd[tok(ym), high].astype(f32) + y1[1].astype(f32)).astype(bf16)
    y2_m = send(yd.at[tok(ym)], y2.at[1], to_ym)
    up_tiles(8, 12)
    y2_p.wait_recv()
    y2_m.wait_recv()
    gi_ref[...] = (
        yd[tok(y), :].astype(f32) + y2[0].astype(f32) + y2[1].astype(f32)
    ).astype(bf16)
    for copy in sent:
        copy.wait_send()
    for store in stores:
        store.wait()


def on_device(layer_input, grad_output, expert_ids, gate_probs, up_weight, down_weight):
    dp = lax.axis_index("dp")
    ex = lax.axis_index("expert")
    y = (dp // 2) * 2 + ex // 4
    flat = expert_ids.T.reshape(-1)
    order = jnp.arange(2 * TOK, dtype=jnp.int32)
    same = (flat[:, None] == flat[None, :]) & (order[:, None] < order[None, :])
    position = jnp.sum(same.astype(jnp.int32), axis=0)
    target = ((flat % 4) * BLOCK + y * CAP + position).astype(f32).reshape(2, TOK)
    parity = (flat // 4).reshape(2, TOK)
    meta = jnp.concatenate(
        [
            jnp.where(parity == 0, target, -1.0),
            jnp.where(parity == 1, target, -1.0),
            gate_probs.T,
            jnp.zeros((2, TOK), f32),
        ],
        axis=0,
    )
    vmem = pl.BlockSpec(memory_space=pltpu.VMEM)
    hbm = pl.BlockSpec(memory_space=pl.ANY)
    return pl.pallas_call(
        kernel,
        out_shape=(
            jax.ShapeDtypeStruct((TOK, QUARTER), bf16),
            jax.ShapeDtypeStruct(up_weight.shape, bf16),
            jax.ShapeDtypeStruct(down_weight.shape, bf16),
        ),
        in_specs=[vmem, vmem, vmem, hbm, hbm],
        out_specs=(vmem, hbm, hbm),
        scratch_shapes=[
            pltpu.VMEM((ROWS, D), bf16),
            pltpu.VMEM((ROWS, D), bf16),
            pltpu.VMEM((D, F), bf16),
            pltpu.VMEM((F, D), bf16),
            pltpu.VMEM((ROWS, F), bf16),
            pltpu.VMEM((ROWS, F), bf16),
            pltpu.VMEM((4 * TOK, QUARTER), bf16),
            pltpu.VMEM((4 * TOK, QUARTER), bf16),
            pltpu.VMEM((4, 8, TOK), f32),
            pltpu.VMEM((4 * BLOCK, 4 * TOK), bf16),
            pltpu.VMEM((4 * BLOCK, QUARTER), bf16),
            pltpu.VMEM((4 * BLOCK, QUARTER), bf16),
            pltpu.VMEM((ROWS, D), bf16),
            pltpu.VMEM((4, BLOCK, D), bf16),
            pltpu.VMEM((4, 2, BLOCK, HALF), bf16),
            pltpu.VMEM((4, 2, BLOCK, QUARTER), bf16),
            pltpu.VMEM((4 * BLOCK, QUARTER), bf16),
            pltpu.VMEM((4 * TOK, QUARTER), bf16),
            pltpu.VMEM((2, TOK, HALF), bf16),
            pltpu.VMEM((2, TOK, QUARTER), bf16),
            pltpu.SemaphoreType.DMA((N_SEMS,)),
            pltpu.SemaphoreType.DMA((N_SEMS,)),
            pltpu.SemaphoreType.DMA((2,)),
            pltpu.SemaphoreType.DMA((8,)),
        ],
        compiler_params=pltpu.CompilerParams(
            collective_id=0, has_side_effects=True, vmem_limit_bytes=63 * 1024 * 1024
        ),
    )(layer_input, grad_output, meta, up_weight, down_weight)


def solution(mesh):
    return jax.shard_map(
        on_device,
        mesh=mesh,
        in_specs=(
            P(("dp", "expert"), "etp"),
            P(("dp", "expert"), "etp"),
            P(("dp", "expert"), None),
            P(("dp", "expert"), None),
            P("expert", None, ("dp", "etp")),
            P("expert", ("dp", "etp"), None),
        ),
        out_specs=(
            P(("dp", "expert"), "etp"),
            P("expert", None, ("dp", "etp")),
            P("expert", ("dp", "etp"), None),
        ),
        check_vma=False,
    )
```

time: 363 us -> 163 us (0.45)
  waiting for transfers between devices: 204 us -> 0 us
  Pallas kernels: 0 us -> 148 us
  matrix products: 74.2 us -> 0 us
  blocking collectives: 27.7 us -> 0 us
  local copies, waits for them, and re-layouts: 33.6 us -> 10.9 us
  between operations: 14 us -> 0.69 us
  starting transfers between devices: 4.86 us -> 0 us
    pallas_call x0 -> x1, Pallas kernels: none -> 148 us  [on_device(): pl.pallas_call(kernel, out_shape=(jax.ShapeDtypeStruct((TOK, QUARTER), bf...]
    all_gather x4 -> x0, waiting for transfers between devices: 126 us -> none  [the longest x1 43.5 us: on_device(): lax.all_gather(rows_g, 'dp', axis=0, tiled=True)]
    reduce_scatter x1 -> x0, waiting for transfers between devices: 77.9 us -> none  [on_device(): lax.psum_scatter(result.reshape(count_blocks * group_rows, quarter).astyp...]
    dot_general x7 -> x0, matrix products: 74.2 us -> none  [the longest x1 19.2 us: on_device(): jnp.einsum('brf,bqf->brq', chosen_rows, chosen_cols, preferred_element_ty...]
    all_to_all x2 -> x0, blocking collectives: 27.7 us -> none  [the longest x1 16.1 us: on_device(): lax.all_to_all(send_x, 'expert', split_axis=0, concat_axis=0, tiled=True)]
    gather x4 -> x0, local copies, waits for them, and re-layouts: 21.2 us -> none  [the longest x1 14.4 us: on_device(): chosen_cols = jnp.take(up_split, block_index % feature_parts, axis=0)]
    unnamed x8 -> x7, local copies, waits for them, and re-layouts: 2.28 us -> 10.8 us
    reshape x6 -> x0, local copies, waits for them, and re-layouts: 5.55 us -> none  [the longest x1 2.58 us: on_device(): rows_x = full_x.reshape(group_rows, quarter * feature_parts)]
  transfers between devices with their start and end apart: 6 -> 0, of which waited for: 5 -> 0; matrix products, arithmetic and copies ran while one was open for 18% -> 0% of each run, Pallas kernels for 0% -> 0%
where the time goes in v1:
time: 163 us; the launch traced here: 162 us
  Pallas kernels  148 us (91%)
  local copies, waits for them, and re-layouts  10.9 us (7%)
  other arithmetic  2.91 us (2%)
    pallas_call x1, Pallas kernels, on_device(): pl.pallas_call(kernel, out_shape=(jax.ShapeDtypeStruct((TOK, QUARTER), bf...  148 us
    unnamed x7, local copies, waits for them, and re-layouts  10.8 us

profile of v1, /device:TPU:0, one launch (start us, length us, event | category | flops | bytes accessed | tf_op | source)
XLA Modules:
  0.0 162.2 jit_solution(1366612953942620647)
XLA Ops:
  0.7 0.1 pad.3.clone
  0.7 0.9 convert_reduce_fusion
  1.6 0.7 compare_select_fusion.1
  2.3 1.3 maximum_maximum_fusion.meta_ref
  3.7 147.7 %shard_map.85 = (bf16[128,768]{1,0:T(8,128)(2,1)}, bf16[1,3072,1024]{2,1,0:T(8,128)(2,1)}, bf16[1,1024,3072]{2,1,0:T(8,128)(2,1)}) custom-call(bf16[128,768]{1,0:T(8,128)(2,1)} %x_ref.1, bf16[128,768]{1,0:T(8,128)(2,1)} %g_ref.1, f32[8,128]{1,0:T(8,128)} %maximum_maximum_fusion.meta_ref, bf16[1,3072,1024]{2,1,0:T(8,128)(2,1)} %up_hbm.1, ...), custom_call_target="tpu_custom_call" | custom-call | tf_op jit(solution)/shard_map/pallas_call | solution.py:363
  151.4 0.0 slice-start
  151.4 1.8 %copy.12 = bf16[128,768]{1,0:T(8,128)(2,1)} copy(bf16[128,768]{1,0:T(8,128)(2,1)} %get-tuple-element.9) | data formatting | bytes 393216
  153.2 0.0 slice-start.1
  153.2 6.3 %copy.13 = bf16[1,3072,1024]{2,1,0:T(8,128)(2,1)} copy(bf16[1,3072,1024]{2,1,0:T(8,128)(2,1)} %get-tuple-element.10) | data formatting | bytes 12582912
  159.5 0.0 slice-done
  159.5 0.0 slice-done.1
  159.5 2.7 %copy.14 = bf16[1,1024,3072]{2,1,0:T(8,128)(2,1)} copy(bf16[1,1024,3072]{2,1,0:T(8,128)(2,1)S(1)} %bitcast.31) | data formatting | bytes 12582912
  (3 shorter events, 0.0 us)
Async XLA Ops:
  151.4 8.1 %slice-start = ((s8[6291456]{0:T(1024)(128)(4,1)}), s8[4194304]{0:T(1024)(128)(4,1)S(1)}, s32[]{:S(2)}) async-start(s8[6291456]{0:T(1024)(128)(4,1)} %bitcast.30), calls=%async_computation | async-start | bytes 8388608
  153.2 6.4 %slice-start.1 = ((s8[6291456]{0:T(1024)(128)(4,1)}), s8[2097152]{0:T(1024)(128)(4,1)S(1)}, s32[]{:S(2)}) async-start(s8[6291456]{0:T(1024)(128)(4,1)} %bitcast.30), calls=%async_computation.1 | async-start | bytes 4194304

commit v2 on v1

v2 whole, which is shorter than its diff:
```python
import jax
import jax.numpy as jnp
from jax import lax
from jax.experimental import pallas as pl
from jax.experimental.pallas import tpu as pltpu
from jax.sharding import PartitionSpec as P

inv_root_two = 0.7071067811865476
inv_root_tau = 0.3989422804014327
MESH = pl.DeviceIdType.MESH
bf16 = jnp.bfloat16
f32 = jnp.float32

TOK = 128
QUARTER = 768
NEAR = 512
FAR = 256
CAP = 36
BLOCK = 4 * CAP
CHUNK = 2 * BLOCK
ROWS = 4 * CHUNK
D = 3072
F = 1024
SPLIT = 4 * NEAR
ALL_FAR = 4 * FAR
TILE = 256
WIDE = 512
FAR_PARTS = (pl.ds(0, ALL_FAR // 2), pl.ds(ALL_FAR // 2, ALL_FAR // 2))
OFFSETS = (0, 3, 1, 2)
N_SEMS = 142
SEND_SEMS = 48


def pieces():
    out = []
    for k in range(4):
        out.append((k * NEAR, k * QUARTER, NEAR))
        out.append((SPLIT + k * FAR, k * QUARTER + NEAR, FAR))
    return out


def kernel(
    x_ref, g_ref, ids_ref, gates_ref, up_hbm, down_hbm,
    gi_ref, gup_hbm, gdown_hbm,
    rows_x, rows_g, up, down, hid, pre, meta, place,
    d1x, d1g, d2x, d2g, p1x, p1g, p2x, p2g,
    dx, r1, r2a, r2b, z1, z2, yd1, yd2, y1a, y1b, y2a, y2b, xsum, xa, xb,
    ssem, rsem, wsem, osem,
):
    dp = lax.axis_index("dp")
    ex = lax.axis_index("expert")
    x = lax.axis_index("etp")
    c = dp % 2
    yl = ex // 4
    z = ex % 4
    y = (dp // 2) * 2 + yl

    def device(x_, y_, z_, c_):
        return ((y_ // 2) * 2 + c_, (y_ % 2) * 4 + z_, x_)

    xp, xm, xo = (x + 1) % 4, (x + 3) % 4, (x + 2) % 4
    yp, ym, yo = (y + 1) % 4, (y + 3) % 4, (y + 2) % 4
    to_xp, to_xm = device(xp, y, z, c), device(xm, y, z, c)
    to_yp, to_ym = device(x, yp, z, c), device(x, ym, z, c)
    to_core = device(x, y, z, 1 - c)
    to_z = {d: device(x, y, (z + d) % 4, c) for d in (1, 2, 3)}

    def span(start, width):
        return pl.ds(pl.multiple_of(start, width), width)

    def tok(y_):
        return span(y_ * TOK, TOK)

    def packed(z_):
        return span(z_ * BLOCK, BLOCK)

    def block(z_, c_):
        return span((z_ * 2 + c_) * BLOCK, BLOCK)

    def chunk(z_):
        return span(z_ * CHUNK, CHUNK)

    def near(x_):
        return span(x_ * NEAR, NEAR)

    def far(x_):
        return span(x_ * FAR, FAR)

    all_near, all_far = slice(0, SPLIT), slice(SPLIT, D)
    sent = []

    def send(src, dst, to):
        i = len(sent)
        if i >= SEND_SEMS:
            sent[i - SEND_SEMS].wait_send()
        copy = pltpu.make_async_remote_copy(
            src_ref=src, dst_ref=dst, send_sem=ssem.at[i % SEND_SEMS], recv_sem=rsem.at[i],
            device_id=to, device_id_type=MESH,
        )
        copy.start()
        sent.append(copy)
        return copy

    def arrived(copies):
        for copy in copies:
            copy.wait_recv()

    def gather(own, into, below, here, above, down_to, up_to):
        one, two = into
        first = (
            send(own[0], one(here), up_to),
            send(own[1], two(here), down_to),
            send(own[0], one(here), down_to),
            send(own[1], two(here), up_to),
        )

        def forward():
            first[0].wait_recv()
            up = send(one(below), one(below), up_to)
            first[1].wait_recv()
            down = send(two(above), two(above), down_to)
            return (first[2], first[3], up, down)

        return forward

    def scatter(at, half, below, here, above, opposite, down_to, up_to, a, b):
        low, high = slice(0, half), slice(half, 2 * half)
        halves = (send(at(opposite, low), a.at[0], up_to), send(at(opposite, high), a.at[1], down_to))

        def middle():
            halves[0].wait_recv()
            ref = at(above, low)
            ref[...] = (ref[...].astype(f32) + a[0].astype(f32)).astype(bf16)
            up = send(at(above, None), b.at[0], up_to)
            halves[1].wait_recv()
            ref = at(below, high)
            ref[...] = (ref[...].astype(f32) + a[1].astype(f32)).astype(bf16)
            down = send(at(below, None), b.at[1], down_to)

            def end():
                arrived((up, down))
                return at(here, None)[...].astype(f32) + b[0].astype(f32) + b[1].astype(f32)

            return end

        return middle

    partners = (to_xp, to_xm, to_yp, to_ym, to_core, to_z[1], to_z[2], to_z[3])
    barrier = pltpu.get_barrier_semaphore()
    for partner in partners:
        pl.semaphore_signal(barrier, inc=1, device_id=partner, device_id_type=MESH)
    pl.semaphore_wait(barrier, len(partners))

    lo, hi = pl.ds(0, NEAR), pl.ds(NEAR, FAR)
    y1_forward = gather(
        (x_ref.at[:, lo], g_ref.at[:, lo]),
        (lambda k: d1x.at[tok(k)], lambda k: d1g.at[tok(k)]),
        ym, y, yp, to_ym, to_yp,
    )
    x2_forward = gather(
        (x_ref.at[:, hi], g_ref.at[:, hi]),
        (lambda k: d2x.at[tok(y), far(k)], lambda k: d2g.at[tok(y), far(k)]),
        xm, x, xp, to_xm, to_xp,
    )
    for there, here, width in pieces():
        pltpu.make_async_copy(
            up_hbm.at[0, pl.ds(here, width), :], up.at[pl.ds(there, width), :], wsem.at[0]
        ).start()
        pltpu.make_async_copy(
            down_hbm.at[0, :, pl.ds(here, width)], down.at[:, pl.ds(there, width)], wsem.at[1]
        ).start()

    ids = ids_ref[...]
    expert = lax.broadcasted_iota(jnp.int32, (8, TOK), 0)
    one = jnp.where(expert == ids[0:1], 1.0, 0.0)
    two = jnp.where(expert == ids[1:2], 1.0, 0.0)
    earlier = (
        lax.broadcasted_iota(jnp.int32, (TOK, TOK), 0) < lax.broadcasted_iota(jnp.int32, (TOK, TOK), 1)
    )
    before = jnp.dot(
        jnp.concatenate([one, two], axis=0).astype(bf16),
        jnp.where(earlier, 1.0, 0.0).astype(bf16),
        preferred_element_type=f32,
    )
    one_at = jnp.sum(before[:8] * one, axis=0, keepdims=True)
    two_at = jnp.sum((before[8:] + jnp.sum(one, axis=1, keepdims=True)) * two, axis=0, keepdims=True)
    upper = ids >= 4
    base = (jnp.where(upper, ids - 4, ids) * BLOCK + y * CAP).astype(f32)
    for k, at in ((0, one_at), (1, two_at)):
        target = base[k:k + 1] + at
        meta[y, k:k + 1] = jnp.where(upper[k:k + 1], -1.0, target)
        meta[y, k + 2:k + 3] = jnp.where(upper[k:k + 1], target, -1.0)
        meta[y, k + 4:k + 5] = gates_ref[k:k + 1, :]
    meta[y, 6:8] = jnp.zeros((2, TOK), f32)
    m_p = send(meta.at[y], meta.at[y], to_yp)
    m_m = send(meta.at[y], meta.at[y], to_ym)
    d1x[tok(y), :] = x_ref[:, lo]
    d1g[tok(y), :] = g_ref[:, lo]
    d2x[tok(y), far(x)] = x_ref[:, hi]
    d2g[tok(y), far(x)] = g_ref[:, hi]

    x2_in = x2_forward()
    y1_in = y1_forward()
    m_p.wait_recv()
    m_f = send(meta.at[ym], meta.at[ym], to_yp)
    arrived(x2_in)

    def y2_gather(cols):
        return gather(
            (d2x.at[tok(y), cols], d2g.at[tok(y), cols]),
            (lambda k: d2x.at[tok(k), cols], lambda k: d2g.at[tok(k), cols]),
            ym, y, yp, to_ym, to_yp,
        )

    y2_forward = [y2_gather(FAR_PARTS[0])]
    arrived((m_m, m_f))
    row = lax.broadcasted_iota(jnp.int32, (4 * BLOCK, TOK), 0).astype(f32)
    gate = jnp.zeros((4 * BLOCK, 1), f32)
    for t in range(4):
        m = meta[t]
        first = row == jnp.where(yl == 0, m[0:1], m[2:3])
        second = row == jnp.where(yl == 0, m[1:2], m[3:4])
        hits = jnp.where(first, 1.0, 0.0) + jnp.where(second, 1.0, 0.0)
        place[:, t * TOK:(t + 1) * TOK] = hits.astype(bf16)
        gates = jnp.where(first, m[4:5], 0.0) + jnp.where(second, m[5:6], 0.0)
        gate = gate + jnp.sum(gates, axis=1, keepdims=True)

    def pack(from_x, from_g, to_x, to_g, cols):
        to_x[:, cols] = jnp.dot(place[...], from_x[:, cols], preferred_element_type=f32).astype(bf16)
        to_g[:, cols] = (
            jnp.dot(place[...], from_g[:, cols], preferred_element_type=f32) * gate
        ).astype(bf16)

    def to_expert(d, from_x, from_g, cols, into):
        there = (packed((z + d) % 4), cols)
        here = (block(z, c), into)
        return (
            send(from_x.at[there], rows_x.at[here], to_z[d]),
            send(from_g.at[there], rows_g.at[here], to_z[d]),
        )

    def keep(from_x, from_g, cols, into):
        here = (block(z, c), into)
        rows_x[here] = from_x[packed(z), cols]
        rows_g[here] = from_g[packed(z), cols]

    zs = [(z + o) % 4 for o in OFFSETS]
    x_in = {}
    near_z = {}
    far_z = {}
    near_in = {}
    far_in = {}
    r1_far = {}
    r1_near = {}
    r2_middle = {}
    r2_end = {}
    z1_in = []
    z2_in = []

    def x_send(j):
        if j > 0:
            arrived(near_z[(4 - OFFSETS[j]) % 4])
        rows = block(zs[j], c)
        x_in[j] = gather(
            (rows_x.at[rows, near(x)], rows_g.at[rows, near(x)]),
            (lambda k: rows_x.at[rows, near(k)], lambda k: rows_g.at[rows, near(k)]),
            xm, x, xp, to_xm, to_xp,
        )

    def x_forward(j):
        x_in[j] = x_in[j]()

    def near_send(j):
        arrived(x_in[j])
        at = (block(zs[j], c), all_near)
        near_in[j] = [send(r.at[at], r.at[at], to_core) for r in (rows_x, rows_g)]

    def far_send(j):
        if j > 0:
            arrived(far_z[(4 - OFFSETS[j]) % 4])
        at = (block(zs[j], c), all_far)
        far_in[j] = [send(r.at[at], r.at[at], to_core) for r in (rows_x, rows_g)]

    def hidden_of(j):
        arrived(near_in[j])
        arrived(far_in[j])
        rows = chunk(zs[j])

        @pl.loop(0, F // WIDE)
        def _(n):
            cols = pl.ds(pl.multiple_of(n * WIDE, WIDE), WIDE)
            act = jnp.dot(rows_x[rows, :], up[:, cols], preferred_element_type=f32)
            back = lax.dot_general(
                rows_g[rows, :], down[cols, :], (((1,), (1,)), ((), ())),
                preferred_element_type=f32,
            )
            half_cdf = 0.5 * (1.0 + lax.erf(act * inv_root_two))
            hid[rows, cols] = (act * half_cdf).astype(bf16)
            slope = half_cdf + act * jnp.exp(-0.5 * act * act) * inv_root_tau
            pre[rows, cols] = (back * slope).astype(bf16)

    def input_grad(j, first, last):
        rows = chunk(zs[j])

        @pl.loop(first, last)
        def _(n):
            cols = pl.ds(pl.multiple_of(n * F, F), F)
            dx[rows, cols] = lax.dot_general(
                pre[rows, :], up[cols, :], (((1,), (1,)), ((), ())),
                preferred_element_type=f32,
            ).astype(bf16)

    def input_grad_of(j):
        input_grad(j, SPLIT // F, D // F)
        r1_far[j] = send(dx.at[block(zs[j], 1 - c), all_far], r1.at[j, :, all_far], to_core)
        input_grad(j, 0, SPLIT // F)
        r1_near[j] = send(dx.at[block(zs[j], 1 - c), all_near], r1.at[j, :, all_near], to_core)

    def add_core(j):
        rows = block(zs[j], c)
        r1_far[j].wait_recv()
        total = (dx[rows, all_far].astype(f32) + r1[j, :, all_far].astype(f32)).astype(bf16)
        if OFFSETS[j] == 0:
            z2[packed(z), :] = total
        else:
            dx[rows, all_far] = total
            z2_in.append(send(dx.at[rows, all_far], z2.at[packed(z)], to_z[OFFSETS[j]]))
        r1_near[j].wait_recv()
        dx[rows, all_near] = (
            dx[rows, all_near].astype(f32) + r1[j, :, all_near].astype(f32)
        ).astype(bf16)

        def at(k, half):
            if half is None:
                return dx.at[rows, near(k)]
            return dx.at[rows, span(k * NEAR + half.start, NEAR // 2)]

        r2_middle[j] = scatter(at, NEAR // 2, xm, x, xp, xo, to_xm, to_xp, r2a.at[j], r2b.at[j])

    def add_far(j):
        r2_end[j] = r2_middle[j]()

    def add_near(j):
        rows = block(zs[j], c)
        total = r2_end[j]().astype(bf16)
        if OFFSETS[j] == 0:
            z1[packed(z), :] = total
        else:
            dx[rows, near(x)] = total
            z1_in.append(send(dx.at[rows, near(x)], z1.at[packed(z)], to_z[OFFSETS[j]]))

    def unpack(rows, tokens):
        tokens[...] = lax.dot_general(
            place[...], rows[...], (((0,), (0,)), ((), ())), preferred_element_type=f32
        ).astype(bf16)

    def over_x(tokens, a, b):
        def at(k, part):
            return tokens.at[:, far(k)] if part is None else tokens.at[:, span(k * FAR + part.start, FAR // 2)]

        return scatter(at, FAR // 2, xm, x, xp, xo, to_xm, to_xp, a, b)

    def over_y(tokens, half, a, b):
        def at(k, part):
            return tokens.at[tok(k)] if part is None else tokens.at[tok(k), part]

        return scatter(at, half, ym, y, yp, yo, to_ym, to_yp, a, b)

    def down_tiles(first, last):
        @pl.loop(first, last)
        def _(u):
            cols = pl.ds(pl.multiple_of(u // 3 * TILE, TILE), TILE)
            wide = pl.ds(pl.multiple_of(u % 3 * F, F), F)
            down[cols, wide] = lax.dot_general(
                hid[:, cols], rows_g[:, wide], (((0,), (0,)), ((), ())),
                preferred_element_type=f32,
            ).astype(bf16)

        for n in range(first // 3, last // 3):
            rows = pl.ds(n * TILE, TILE)
            for there, here, width in pieces():
                pltpu.make_async_copy(
                    down.at[rows, pl.ds(there, width)], gdown_hbm.at[0, rows, pl.ds(here, width)], osem.at[1]
                ).start()

    def up_tiles(first, last):
        @pl.loop(first, last)
        def _(n):
            cols = pl.ds(pl.multiple_of(n * TILE, TILE), TILE)
            up[cols, :] = lax.dot_general(
                rows_x[:, cols], pre[...], (((0,), (0,)), ((), ())),
                preferred_element_type=f32,
            ).astype(bf16)

        for there, here, width in pieces():
            for t in range(0, width, TILE):
                if first * TILE <= there + t < last * TILE:
                    pltpu.make_async_copy(
                        up.at[pl.ds(there + t, TILE)], gup_hbm.at[0, pl.ds(here + t, TILE)], osem.at[0]
                    ).start()

    def near_to(d):
        near_z[d] = to_expert(d, p1x, p1g, pl.ds(0, NEAR), near(x))

    def far_to(d, part):
        into = pl.ds(SPLIT + part * (ALL_FAR // 2), ALL_FAR // 2)
        far_z[d] = far_z.get(d, ()) + to_expert(d, p2x, p2g, FAR_PARTS[part], into)

    def far_pack(part):
        pack(d2x, d2g, p2x, p2g, FAR_PARTS[part])
        far_to(1, part)
        far_to(3, part)
        keep(p2x, p2g, FAR_PARTS[part], pl.ds(SPLIT + part * (ALL_FAR // 2), ALL_FAR // 2))

    arrived(y1_in)
    pack(d1x, d1g, p1x, p1g, pl.ds(0, NEAR))
    near_to(1)
    near_to(3)
    keep(p1x, p1g, pl.ds(0, NEAR), near(x))
    x_send(0)
    y2_first = y2_forward[0]()
    y2_second = y2_gather(FAR_PARTS[1])
    x_send(1)
    near_to(2)
    x_forward(0)
    arrived(y2_first)
    far_pack(0)
    x_send(2)
    y2_second = y2_second()
    x_forward(1)
    arrived(y2_second)
    far_pack(1)
    near_send(0)
    far_send(0)
    far_to(2, 0)
    far_to(2, 1)
    x_send(3)
    pltpu.make_async_copy(up_hbm.at[0], up, wsem.at[0]).wait()
    pltpu.make_async_copy(down_hbm.at[0], down, wsem.at[1]).wait()
    hidden_of(0)
    x_forward(2)
    near_send(1)
    input_grad_of(0)
    far_send(1)
    x_forward(3)
    add_core(0)
    near_send(2)
    hidden_of(1)
    far_send(2)
    add_far(0)
    input_grad_of(1)
    near_send(3)
    add_core(1)
    hidden_of(2)
    far_send(3)
    add_near(0)
    add_far(1)
    input_grad_of(2)
    add_core(2)
    add_near(1)
    hidden_of(3)
    add_far(2)
    input_grad_of(3)
    add_near(2)
    down_tiles(0, 2)
    add_core(3)
    down_tiles(2, 5)
    add_far(3)
    down_tiles(5, 8)
    add_near(3)
    arrived(z2_in)
    unpack(z2, yd2)
    x_middle = over_x(yd2, xa, xb)
    down_tiles(8, 12)
    x_end = x_middle()
    arrived(z1_in)
    unpack(z1, yd1)
    near_middle = over_y(yd1, NEAR // 2, y1a, y1b)
    up_tiles(0, 3)
    near_end = near_middle()
    up_tiles(3, 5)
    xsum[...] = x_end().astype(bf16)
    far_middle = over_y(xsum, FAR // 2, y2a, y2b)
    up_tiles(5, 8)
    far_end = far_middle()
    up_tiles(8, 12)
    gi_ref[:, lo] = near_end().astype(bf16)
    gi_ref[:, hi] = far_end().astype(bf16)
    for copy in sent[-SEND_SEMS:]:
        copy.wait_send()
    pltpu.make_async_copy(up, gup_hbm.at[0], osem.at[0]).wait()
    pltpu.make_async_copy(down, gdown_hbm.at[0], osem.at[1]).wait()


def on_device(layer_input, grad_output, expert_ids, gate_probs, up_weight, down_weight):
    vmem = pl.BlockSpec(memory_space=pltpu.VMEM)
    hbm = pl.BlockSpec(memory_space=pl.ANY)

    def buf(*shape):
        return pltpu.VMEM(shape, bf16)

    return pl.pallas_call(
        kernel,
        out_shape=(
            jax.ShapeDtypeStruct((TOK, QUARTER), bf16),
            jax.ShapeDtypeStruct(up_weight.shape, bf16),
            jax.ShapeDtypeStruct(down_weight.shape, bf16),
        ),
        in_specs=[vmem, vmem, vmem, vmem, hbm, hbm],
        out_specs=(vmem, hbm, hbm),
        scratch_shapes=[
            buf(ROWS, D),
            buf(ROWS, D),
            buf(D, F),
            buf(F, D),
            buf(ROWS, F),
            buf(ROWS, F),
            pltpu.VMEM((4, 8, TOK), f32),
            buf(4 * BLOCK, 4 * TOK),
            buf(4 * TOK, NEAR),
            buf(4 * TOK, NEAR),
            buf(4 * TOK, ALL_FAR),
            buf(4 * TOK, ALL_FAR),
            buf(4 * BLOCK, NEAR),
            buf(4 * BLOCK, NEAR),
            buf(4 * BLOCK, ALL_FAR),
            buf(4 * BLOCK, ALL_FAR),
            buf(ROWS, D),
            buf(4, BLOCK, D),
            buf(4, 2, BLOCK, NEAR // 2),
            buf(4, 2, BLOCK, NEAR),
            buf(4 * BLOCK, NEAR),
            buf(4 * BLOCK, ALL_FAR),
            buf(4 * TOK, NEAR),
            buf(4 * TOK, ALL_FAR),
            buf(2, TOK, NEAR // 2),
            buf(2, TOK, NEAR),
            buf(2, TOK, FAR // 2),
            buf(2, TOK, FAR),
            buf(4 * TOK, FAR),
            buf(2, 4 * TOK, FAR // 2),
            buf(2, 4 * TOK, FAR),
            pltpu.SemaphoreType.DMA((SEND_SEMS,)),
            pltpu.SemaphoreType.DMA((N_SEMS,)),
            pltpu.SemaphoreType.DMA((2,)),
            pltpu.SemaphoreType.DMA((2,)),
        ],
        compiler_params=pltpu.CompilerParams(
            collective_id=0, has_side_effects=True, vmem_limit_bytes=63 * 1024 * 1024
        ),
    )(layer_input, grad_output, expert_ids.T, gate_probs.T, up_weight, down_weight)


def solution(mesh):
    return jax.shard_map(
        on_device,
        mesh=mesh,
        in_specs=(
            P(("dp", "expert"), "etp"),
            P(("dp", "expert"), "etp"),
            P(("dp", "expert"), None),
            P(("dp", "expert"), None),
            P("expert", None, ("dp", "etp")),
            P("expert", ("dp", "etp"), None),
        ),
        out_specs=(
            P(("dp", "expert"), "etp"),
            P("expert", None, ("dp", "etp")),
            P("expert", ("dp", "etp"), None),
        ),
        check_vma=False,
    )
```

time: 163 us -> 137 us (0.84)
  Pallas kernels: 148 us -> 125 us
  other arithmetic: 2.91 us -> 0.01 us
    pallas_call x1, Pallas kernels: 148 us -> 125 us  [on_device(): pl.pallas_call(kernel, out_shape=(jax.ShapeDtypeStruct((TOK, QUARTER), bf...]
where the time goes in v2:
time: 137 us
  Pallas kernels  125 us (91%)
  local copies, waits for them, and re-layouts  10.8 us (8%)
    pallas_call x1, Pallas kernels, on_device(): pl.pallas_call(kernel, out_shape=(jax.ShapeDtypeStruct((TOK, QUARTER), bf...  125 us
    unnamed x7, local copies, waits for them, and re-layouts  10.8 us

profile of v2, /device:TPU:0, one launch (start us, length us, event | category | flops | bytes accessed | tf_op | source)
XLA Modules:
  0.0 136.7 jit_solution(10325515153574879690)
XLA Ops:
  0.6 125.2 %shard_map.85 = (bf16[128,768]{1,0:T(8,128)(2,1)}, bf16[1,3072,1024]{2,1,0:T(8,128)(2,1)}, bf16[1,1024,3072]{2,1,0:T(8,128)(2,1)}) custom-call(bf16[128,768]{1,0:T(8,128)(2,1)} %x_ref.1, bf16[128,768]{1,0:T(8,128)(2,1)} %g_ref.1, s32[2,128]{1,0:T(2,128)} %bitcast.4, f32[2,128]{1,0:T(2,128)} %bitcast.5, bf16[1,3072,1024]{2,1,0:T(8,128)(2,1)} %up_hbm.1, ...), custom_call_target="tpu_custom_call" | custom-call | tf_op jit(solution)/shard_map/pallas_call | solution.py:502
  125.9 0.0 slice-start
  125.9 1.8 %copy.12 = bf16[128,768]{1,0:T(8,128)(2,1)} copy(bf16[128,768]{1,0:T(8,128)(2,1)} %get-tuple-element.6) | data formatting | bytes 393216
  127.6 0.0 slice-start.1
  127.6 6.3 %copy.13 = bf16[1,3072,1024]{2,1,0:T(8,128)(2,1)} copy(bf16[1,3072,1024]{2,1,0:T(8,128)(2,1)} %get-tuple-element.7) | data formatting | bytes 12582912
  134.0 0.0 slice-done
  134.0 0.0 slice-done.1
  134.0 2.7 %copy.14 = bf16[1,1024,3072]{2,1,0:T(8,128)(2,1)} copy(bf16[1,1024,3072]{2,1,0:T(8,128)(2,1)S(1)} %bitcast.3) | data formatting | bytes 12582912
  (1 shorter events, 0.0 us)
Async XLA Ops:
  125.9 8.1 %slice-start = ((s8[6291456]{0:T(1024)(128)(4,1)}), s8[4194304]{0:T(1024)(128)(4,1)S(1)}, s32[]{:S(2)}) async-start(s8[6291456]{0:T(1024)(128)(4,1)} %bitcast.2), calls=%async_computation | async-start | bytes 8388608
  127.6 6.4 %slice-start.1 = ((s8[6291456]{0:T(1024)(128)(4,1)}), s8[2097152]{0:T(1024)(128)(4,1)S(1)}, s32[]{:S(2)}) async-start(s8[6291456]{0:T(1024)(128)(4,1)} %bitcast.2), calls=%async_computation.1 | async-start | bytes 4194304

commit v3 on v2

--- a/solution.py
+++ b/solution.py
@@ -27,7 +27,7 @@
 WIDE = 512
 FAR_PARTS = (pl.ds(0, ALL_FAR // 2), pl.ds(ALL_FAR // 2, ALL_FAR // 2))
 OFFSETS = (0, 3, 1, 2)
-N_SEMS = 142
+N_SEMS = 144
 SEND_SEMS = 48
 
 
@@ -41,12 +41,13 @@
 
 def kernel(
     x_ref, g_ref, ids_ref, gates_ref, up_hbm, down_hbm,
-    gi_ref, gup_hbm, gdown_hbm,
-    rows_x, rows_g, up, down, hid, pre, meta, place,
+    gi_ref, gup_ref, gdown_ref,
+    rows_x, rows_g, hid, pre, meta, place,
     d1x, d1g, d2x, d2g, p1x, p1g, p2x, p2g,
     dx, r1, r2a, r2b, z1, z2, yd1, yd2, y1a, y1b, y2a, y2b, xsum, xa, xb,
-    ssem, rsem, wsem, osem,
+    ssem, rsem, wsem,
 ):
+    up, down = gup_ref.at[0], gdown_ref.at[0]
     dp = lax.axis_index("dp")
     ex = lax.axis_index("expert")
     x = lax.axis_index("etp")
@@ -275,18 +276,23 @@
         at = (block(zs[j], c), all_near)
         near_in[j] = [send(r.at[at], r.at[at], to_core) for r in (rows_x, rows_g)]
 
+    def far_part_send(j, part):
+        at = (block(zs[j], c), pl.ds(SPLIT + part * (ALL_FAR // 2), ALL_FAR // 2))
+        far_in[j] = far_in.get(j, []) + [send(r.at[at], r.at[at], to_core) for r in (rows_x, rows_g)]
+
     def far_send(j):
         if j > 0:
             arrived(far_z[(4 - OFFSETS[j]) % 4])
         at = (block(zs[j], c), all_far)
         far_in[j] = [send(r.at[at], r.at[at], to_core) for r in (rows_x, rows_g)]
 
-    def hidden_of(j):
-        arrived(near_in[j])
-        arrived(far_in[j])
+    def hidden_of(j, first, last):
+        if first == 0:
+            arrived(near_in[j])
+            arrived(far_in[j])
         rows = chunk(zs[j])
 
-        @pl.loop(0, F // WIDE)
+        @pl.loop(first, last)
         def _(n):
             cols = pl.ds(pl.multiple_of(n * WIDE, WIDE), WIDE)
             act = jnp.dot(rows_x[rows, :], up[:, cols], preferred_element_type=f32)
@@ -366,38 +372,33 @@
 
         return scatter(at, half, ym, y, yp, yo, to_ym, to_yp, a, b)
 
-    def down_tiles(first, last):
+    def down_tiles(k, first, last):
+        wide = slice(k * F, (k + 1) * F)
+
         @pl.loop(first, last)
-        def _(u):
-            cols = pl.ds(pl.multiple_of(u // 3 * TILE, TILE), TILE)
-            wide = pl.ds(pl.multiple_of(u % 3 * F, F), F)
-            down[cols, wide] = lax.dot_general(
+        def _(n):
+            cols = pl.ds(pl.multiple_of(n * TILE, TILE), TILE)
+            part = lax.dot_general(
                 hid[:, cols], rows_g[:, wide], (((0,), (0,)), ((), ())),
                 preferred_element_type=f32,
             ).astype(bf16)
-
-        for n in range(first // 3, last // 3):
-            rows = pl.ds(n * TILE, TILE)
             for there, here, width in pieces():
-                pltpu.make_async_copy(
-                    down.at[rows, pl.ds(there, width)], gdown_hbm.at[0, rows, pl.ds(here, width)], osem.at[1]
-                ).start()
+                if wide.start <= there < wide.stop:
+                    start = there - wide.start
+                    down[cols, pl.ds(here, width)] = part[:, start:start + width]
 
     def up_tiles(first, last):
         @pl.loop(first, last)
         def _(n):
             cols = pl.ds(pl.multiple_of(n * TILE, TILE), TILE)
-            up[cols, :] = lax.dot_general(
+            if last * TILE <= SPLIT:
+                here = n // 2 * QUARTER + n % 2 * TILE
+            else:
+                here = (n - SPLIT // TILE) * QUARTER + NEAR
+            up[pl.ds(pl.multiple_of(here, TILE), TILE), :] = lax.dot_general(
                 rows_x[:, cols], pre[...], (((0,), (0,)), ((), ())),
                 preferred_element_type=f32,
             ).astype(bf16)
-
-        for there, here, width in pieces():
-            for t in range(0, width, TILE):
-                if first * TILE <= there + t < last * TILE:
-                    pltpu.make_async_copy(
-                        up.at[pl.ds(there + t, TILE)], gup_hbm.at[0, pl.ds(here + t, TILE)], osem.at[0]
-                    ).start()
 
     def near_to(d):
         near_z[d] = to_expert(d, p1x, p1g, pl.ds(0, NEAR), near(x))
@@ -420,58 +421,63 @@
     x_send(0)
     y2_first = y2_forward[0]()
     y2_second = y2_gather(FAR_PARTS[1])
-    x_send(1)
-    near_to(2)
     x_forward(0)
     arrived(y2_first)
     far_pack(0)
+    far_part_send(0, 0)
+    x_send(1)
+    near_to(2)
+    y2_second = y2_second()
     x_send(2)
-    y2_second = y2_second()
-    x_forward(1)
+    near_send(0)
     arrived(y2_second)
     far_pack(1)
-    near_send(0)
-    far_send(0)
+    far_part_send(0, 1)
     far_to(2, 0)
     far_to(2, 1)
+    x_forward(1)
     x_send(3)
     pltpu.make_async_copy(up_hbm.at[0], up, wsem.at[0]).wait()
     pltpu.make_async_copy(down_hbm.at[0], down, wsem.at[1]).wait()
-    hidden_of(0)
+    hidden_of(0, 0, 2)
+    near_send(1)
     x_forward(2)
-    near_send(1)
     input_grad_of(0)
     far_send(1)
+    hidden_of(1, 0, 1)
+    add_core(0)
     x_forward(3)
-    add_core(0)
     near_send(2)
-    hidden_of(1)
+    hidden_of(1, 1, 2)
     far_send(2)
+    input_grad_of(1)
     add_far(0)
-    input_grad_of(1)
     near_send(3)
+    hidden_of(2, 0, 1)
     add_core(1)
-    hidden_of(2)
+    hidden_of(2, 1, 2)
     far_send(3)
     add_near(0)
+    input_grad_of(2)
     add_far(1)
-    input_grad_of(2)
+    hidden_of(3, 0, 1)
     add_core(2)
     add_near(1)
-    hidden_of(3)
+    hidden_of(3, 1, 2)
     add_far(2)
     input_grad_of(3)
     add_near(2)
-    down_tiles(0, 2)
+    down_tiles(0, 0, 2)
     add_core(3)
-    down_tiles(2, 5)
+    down_tiles(0, 2, 4)
+    down_tiles(1, 0, 1)
     add_far(3)
-    down_tiles(5, 8)
+    down_tiles(1, 1, 4)
     add_near(3)
     arrived(z2_in)
     unpack(z2, yd2)
     x_middle = over_x(yd2, xa, xb)
-    down_tiles(8, 12)
+    down_tiles(2, 0, 4)
     x_end = x_middle()
     arrived(z1_in)
     unpack(z1, yd1)
@@ -488,8 +494,6 @@
     gi_ref[:, hi] = far_end().astype(bf16)
     for copy in sent[-SEND_SEMS:]:
         copy.wait_send()
-    pltpu.make_async_copy(up, gup_hbm.at[0], osem.at[0]).wait()
-    pltpu.make_async_copy(down, gdown_hbm.at[0], osem.at[1]).wait()
 
 
 def on_device(layer_input, grad_output, expert_ids, gate_probs, up_weight, down_weight):
@@ -503,16 +507,14 @@
         kernel,
         out_shape=(
             jax.ShapeDtypeStruct((TOK, QUARTER), bf16),
-            jax.ShapeDtypeStruct(up_weight.shape, bf16),
-            jax.ShapeDtypeStruct(down_weight.shape, bf16),
+            pltpu.VMEM(up_weight.shape, bf16),
+            pltpu.VMEM(down_weight.shape, bf16),
         ),
         in_specs=[vmem, vmem, vmem, vmem, hbm, hbm],
-        out_specs=(vmem, hbm, hbm),
+        out_specs=(vmem, vmem, vmem),
         scratch_shapes=[
             buf(ROWS, D),
             buf(ROWS, D),
-            buf(D, F),
-            buf(F, D),
             buf(ROWS, F),
             buf(ROWS, F),
             pltpu.VMEM((4, 8, TOK), f32),
@@ -543,10 +545,9 @@
             pltpu.SemaphoreType.DMA((SEND_SEMS,)),
             pltpu.SemaphoreType.DMA((N_SEMS,)),
             pltpu.SemaphoreType.DMA((2,)),
-            pltpu.SemaphoreType.DMA((2,)),
         ],
         compiler_params=pltpu.CompilerParams(
-            collective_id=0, has_side_effects=True, vmem_limit_bytes=63 * 1024 * 1024
+            collective_id=0, has_side_effects=True, vmem_limit_bytes=51 * 1024 * 1024
         ),
     )(layer_input, grad_output, expert_ids.T, gate_probs.T, up_weight, down_weight)
 

time: 137 us -> 131 us (0.956)
  local copies, waits for them, and re-layouts: 10.8 us -> 6.09 us
    unnamed x7 -> x5, local copies, waits for them, and re-layouts: 10.8 us -> 6.09 us
where the time goes in v3:
time: 131 us
  Pallas kernels  124 us (95%)
  local copies, waits for them, and re-layouts  6.09 us (5%)
    pallas_call x1, Pallas kernels, on_device(): pl.pallas_call(kernel, out_shape=(jax.ShapeDtypeStruct((TOK, QUARTER), bf...  124 us
    unnamed x5, local copies, waits for them, and re-layouts  6.09 us

profile of v3, /device:TPU:0, one launch (start us, length us, event | category | flops | bytes accessed | tf_op | source)
XLA Modules:
  0.0 130.6 jit_solution(14539819549045433136)
XLA Ops:
  0.6 123.9 %shard_map.85 = (bf16[128,768]{1,0:T(8,128)(2,1)}, bf16[1,3072,1024]{2,1,0:T(8,128)(2,1)S(1)}, bf16[1,1024,3072]{2,1,0:T(8,128)(2,1)S(1)}) custom-call(bf16[128,768]{1,0:T(8,128)(2,1)} %x_ref.1, bf16[128,768]{1,0:T(8,128)(2,1)} %g_ref.1, s32[2,128]{1,0:T(2,128)} %bitcast.2, f32[2,128]{1,0:T(2,128)} %bitcast.3, bf16[1,3072,1024]{2,1,0:T(8,128)(2,1)} %up_hbm.1, ...), custom_call_target="tpu_custom_call" | custom-call | tf_op jit(solution)/shard_map/pallas_call | solution.py:506
  124.5 2.7 %copy.12 = bf16[1,3072,1024]{2,1,0:T(8,128)(2,1)} copy(bf16[1,3072,1024]{2,1,0:T(8,128)(2,1)S(1)} %get-tuple-element.4) | data formatting | bytes 12582912
  127.2 0.0 copy-start
  127.2 2.7 %copy.13 = bf16[1,1024,3072]{2,1,0:T(8,128)(2,1)} copy(bf16[1,1024,3072]{2,1,0:T(8,128)(2,1)S(1)} %get-tuple-element.5) | data formatting | bytes 12582912
  129.9 0.0 copy-done
  129.9 0.7 copy.14
Async XLA Ops:
  127.2 2.7 %copy-start = (bf16[128,768]{1,0:T(8,128)(2,1)S(1)}, bf16[128,768]{1,0:T(8,128)(2,1)}, u32[]{:S(2)}) copy-start(bf16[128,768]{1,0:T(8,128)(2,1)} %get-tuple-element.9) | copy-start | bytes 589828

commit v4 on v3

--- a/solution.py
+++ b/solution.py
@@ -466,13 +466,11 @@
     hidden_of(3, 1, 2)
     add_far(2)
     input_grad_of(3)
+    add_core(3)
     add_near(2)
-    down_tiles(0, 0, 2)
-    add_core(3)
-    down_tiles(0, 2, 4)
-    down_tiles(1, 0, 1)
+    down_tiles(0, 0, 4)
     add_far(3)
-    down_tiles(1, 1, 4)
+    down_tiles(1, 0, 4)
     add_near(3)
     arrived(z2_in)
     unpack(z2, yd2)

time: 131 us -> 129 us (0.985)
  Pallas kernels: 124 us -> 122 us
    pallas_call x1, Pallas kernels: 124 us -> 122 us  [on_device(): pl.pallas_call(kernel, out_shape=(jax.ShapeDtypeStruct((TOK, QUARTER), bf...]
where the time goes in v4:
time: 129 us
  Pallas kernels  122 us (95%)
  local copies, waits for them, and re-layouts  6.09 us (5%)
    pallas_call x1, Pallas kernels, on_device(): pl.pallas_call(kernel, out_shape=(jax.ShapeDtypeStruct((TOK, QUARTER), bf...  122 us
    unnamed x5, local copies, waits for them, and re-layouts  6.09 us

profile of v4, /device:TPU:0, one launch (start us, length us, event | category | flops | bytes accessed | tf_op | source)
XLA Modules:
  0.0 128.9 jit_solution(16034238192751416810)
XLA Ops:
  0.6 122.2 %shard_map.85 = (bf16[128,768]{1,0:T(8,128)(2,1)}, bf16[1,3072,1024]{2,1,0:T(8,128)(2,1)S(1)}, bf16[1,1024,3072]{2,1,0:T(8,128)(2,1)S(1)}) custom-call(bf16[128,768]{1,0:T(8,128)(2,1)} %x_ref.1, bf16[128,768]{1,0:T(8,128)(2,1)} %g_ref.1, s32[2,128]{1,0:T(2,128)} %bitcast.2, f32[2,128]{1,0:T(2,128)} %bitcast.3, bf16[1,3072,1024]{2,1,0:T(8,128)(2,1)} %up_hbm.1, ...), custom_call_target="tpu_custom_call" | custom-call | tf_op jit(solution)/shard_map/pallas_call | solution.py:504
  122.8 2.7 %copy.12 = bf16[1,3072,1024]{2,1,0:T(8,128)(2,1)} copy(bf16[1,3072,1024]{2,1,0:T(8,128)(2,1)S(1)} %get-tuple-element.4) | data formatting | bytes 12582912
  125.5 0.0 copy-start
  125.5 2.7 %copy.13 = bf16[1,1024,3072]{2,1,0:T(8,128)(2,1)} copy(bf16[1,1024,3072]{2,1,0:T(8,128)(2,1)S(1)} %get-tuple-element.5) | data formatting | bytes 12582912
  128.2 0.0 copy-done
  128.2 0.7 copy.14
Async XLA Ops:
  125.5 2.7 %copy-start = (bf16[128,768]{1,0:T(8,128)(2,1)S(1)}, bf16[128,768]{1,0:T(8,128)(2,1)}, u32[]{:S(2)}) copy-start(bf16[128,768]{1,0:T(8,128)(2,1)} %get-tuple-element.9) | copy-start | bytes 589828
